TPU v7x, 32 devices: a whole 2x2x4 slice. The times are simulated.
32 devices in a mesh: vol: 4 (over x, core), surf: 8 (over z, y).
Axes of the slice: x: 2, y: 2, z: 4, core: 2. Of those that a mesh axis runs over, the one named last changes fastest.
Arguments:
- points: float32 [3, 4096], P(None, ('vol', 'surf')), may hold values from -1 to 1
- surface_points: float32 [3, 8192], P(None, 'surf'), may hold values from -1 to 1
- displacement: float32 [3, 8192], P(None, 'surf'), may hold values from -6 to 6
- rotation: float32 [3, 8192], P(None, 'surf'), may hold values from -3 to 3
- halo_index: int32 [1024], P(('vol', 'surf')), may hold values from 0 to 127
- connectivity: int32 [4, 16384], P(None, ('vol', 'surf')), may hold values from 0 to 191
Outputs:
- node_motion: float32 [3, 4096], P(None, ('vol', 'surf'))
- swept: float32 [16384], P(('vol', 'surf'))
All inputs are finite; a program needn't handle non-finite values.
Results may differ from a plain program's by a relative error of at most 0.0003.
Values sent between devices are 32-bit elements; how exact they have to be, the bound alone decides.
A program may use at most 64 MiB of HBM per device.

v0:
```python
import functools

import jax
import jax.numpy as jnp
from jax import lax
from jax.experimental import pallas as pl
from jax.experimental.pallas import tpu as pltpu
from jax.sharding import PartitionSpec as P

SOFTENING = 0.01
LANES = 128
ROWS = 8
CHUNK = 256
STEP = 32
FACES = ((1, 2, 3), (0, 3, 2), (0, 1, 3), (0, 2, 1))
MESH = pl.DeviceIdType.MESH


def cross(a, b):
    return (
        a[1] * b[2] - a[2] * b[1],
        a[2] * b[0] - a[0] * b[2],
        a[0] * b[1] - a[1] * b[0],
    )


def split_rows(rows):
    first = rows.astype(jnp.bfloat16)
    rest = rows - first.astype(jnp.float32)
    second = rest.astype(jnp.bfloat16)
    third = rest - second.astype(jnp.float32)
    return jnp.concatenate(
        [first.astype(jnp.float32), second.astype(jnp.float32), third, jnp.zeros_like(rows)], axis=0
    ).astype(jnp.bfloat16)


def pick(rows, index):
    return jnp.take_along_axis(rows, index, axis=1)


def node_shift(totals, rows):
    turn = cross((totals[3:4], totals[4:5], totals[5:6]), (rows[0:1], rows[1:2], rows[2:3]))
    scale = 1.0 / totals[6:7]
    return tuple((totals[k : k + 1] + turn[k]) * scale for k in range(3))


def kernel(
    tiles,
    parts,
    width,
    points_in,
    surface_in,
    displacement_in,
    rotation_in,
    halo_in,
    cells_in,
    result_ref,
    points_ref,
    surface_ref,
    displacement_ref,
    rotation_ref,
    halo_ref,
    cells_ref,
    nodes,
    anchors,
    terms,
    high,
    low,
    partial,
    lent,
    got_own,
    got_before,
    got_after,
    load_sems,
    node_send_sems,
    node_recv_sems,
    send_sems,
    recv_sems,
):
    tile = lax.axis_index("vol")
    me = lax.axis_index("surf")
    before = lax.rem(tile + tiles - 1, tiles)
    after = lax.rem(tile + 1, tiles)
    is_first = me == 0
    is_last = me == parts - 1

    sources = (points_in, halo_in, surface_in, rotation_in, displacement_in, cells_in)
    targets = (points_ref, halo_ref, surface_ref, rotation_ref, displacement_ref, cells_ref)
    loads = [
        pltpu.make_async_copy(source, target, load_sems.at[k])
        for k, (source, target) in enumerate(zip(sources, targets))
    ]
    for load in loads:
        load.start()

    def bulk(ref, count, sem):
        return pltpu.make_async_copy(ref.at[pl.ds(0, count)], ref.at[pl.ds(0, count)], sem)

    def remote(src, dst, send_sem, recv_sem, device):
        return pltpu.make_async_remote_copy(
            src_ref=src,
            dst_ref=dst,
            send_sem=send_sem,
            recv_sem=recv_sem,
            device_id=device,
            device_id_type=MESH,
        )

    barrier = pltpu.get_barrier_semaphore()

    def greet(step, _):
        other = lax.rem(me + step, parts)
        pl.semaphore_signal(barrier, inc=1, device_id=(tile, other), device_id_type=MESH)
        return 0

    def greet_far(far):
        def body(other, _):
            pl.semaphore_signal(barrier, inc=1, device_id=(far, other), device_id_type=MESH)
            return 0

        lax.fori_loop(0, parts, body, 0)

    lax.fori_loop(1, parts, greet, 0)

    @pl.when(is_first)
    def _():
        greet_far(before)

    @pl.when(is_last)
    def _():
        greet_far(after)

    loads[0].wait()
    loads[1].wait()
    halo = halo_ref[...].astype(jnp.float32)
    halo_row = jnp.concatenate([halo] * (LANES // width), axis=1)
    mine = jnp.concatenate(
        [points_ref[...], halo_row, jnp.zeros((ROWS - 4, LANES), jnp.float32)], axis=0
    )
    nodes[me] = mine
    pl.semaphore_wait(barrier, parts + 1)

    def share(step, _):
        other = lax.rem(me + step, parts)
        remote(
            nodes.at[me], nodes.at[me], node_send_sems.at[0], node_recv_sems.at[me], (tile, other)
        ).start()
        return 0

    lax.fori_loop(1, parts, share, 0)

    def share_far(slot, device):
        remote(
            nodes.at[me], nodes.at[slot], node_send_sems.at[1], node_recv_sems.at[slot], device
        ).start()

    @pl.when(is_last)
    def _():
        share_far(parts, (after, 0))

    @pl.when(is_first)
    def _():
        share_far(parts + 1, (before, parts - 1))

    for load in loads[2:5]:
        load.wait()
    depth = surface_ref.shape[1]
    surface = surface_ref[...]
    rotation = rotation_ref[...]
    turned = cross(
        tuple(rotation[k : k + 1] for k in range(3)), tuple(surface[k : k + 1] for k in range(3))
    )
    rows = jnp.concatenate(
        [
            displacement_ref[...] - jnp.concatenate(turned, axis=0),
            rotation,
            jnp.ones((1, depth), jnp.float32),
            jnp.zeros((1, depth), jnp.float32),
        ],
        axis=0,
    )
    terms[...] = split_rows(rows)
    padded = jnp.concatenate([surface, jnp.zeros((ROWS - 3, depth), jnp.float32)], axis=0)
    for start in range(0, depth, LANES):
        upright = padded[:, start : start + LANES].T
        for k in range(3):
            anchors[k, start : start + LANES] = jnp.broadcast_to(
                upright[:, k : k + 1], (LANES, LANES)
            )

    def lent_of(values, slot):
        index = jnp.broadcast_to(nodes[slot][3:4], (ROWS, LANES)).astype(jnp.int32)
        return pick(values, index)

    pair = 2 if parts % 2 == 0 else 1
    pairs = parts // pair
    turn = 1 - 2 * jnp.minimum((me // pair) // max(pairs // 2, 1), 1)

    def sums(step, _):
        base = lax.rem(me // pair + turn * step + pairs, pairs) * pair
        for k in range(pair):

            @pl.when(base + k != me)
            def _():
                pltpu.make_async_copy(
                    nodes.at[base + k], nodes.at[base + k], node_recv_sems.at[base + k]
                ).wait()

        places = [nodes[base + k] for k in range(pair)]
        total = jnp.zeros((4 * ROWS, pair * LANES), jnp.float32)
        for start in range(0, depth, CHUNK):
            for row in range(start, start + CHUNK, STEP):
                cut = slice(row, row + STEP)
                sx, sy, sz = anchors[0, cut], anchors[1, cut], anchors[2, cut]
                for k in range(pair):
                    gx = sx - places[k][0:1]
                    gy = sy - places[k][1:2]
                    gz = sz - places[k][2:3]
                    root = lax.rsqrt(gx * gx + gy * gy + (gz * gz + SOFTENING))
                    weight = root * root * root
                    top = weight.astype(jnp.bfloat16)
                    side = slice(k * LANES, (k + 1) * LANES)
                    high[cut, side] = top
                    low[cut, side] = (weight - top.astype(jnp.float32)).astype(jnp.bfloat16)
            cut = slice(start, start + CHUNK)
            left = terms[:, cut]
            total = total + jnp.dot(left, high[cut], preferred_element_type=jnp.float32)
            total = total + jnp.dot(left, low[cut], preferred_element_type=jnp.float32)
        added = total[0:ROWS] + total[ROWS : 2 * ROWS] + total[2 * ROWS : 3 * ROWS]
        halves = [added[:, k * LANES : (k + 1) * LANES] for k in range(pair)]
        for k in range(pair):
            partial[base + k] = halves[k]
        for k in range(pair):
            lent[base + k] = lent_of(halves[k], base + k)
        for k in range(pair):
            block = base + k
            is_mine = block == me

            @pl.when(is_mine)
            def _():
                got_own[me] = halves[k]

            @pl.when(jnp.logical_not(is_mine))
            def _():
                remote(
                    partial.at[block], got_own.at[me], send_sems.at[0], recv_sems.at[0], (tile, block)
                ).start()

            is_end = block == parts - 1
            owner = (jnp.where(is_end, after, tile), jnp.where(is_end, 0, block + 1))

            @pl.when(block + 1 == me)
            def _():
                got_before[me] = lent[block]

            @pl.when(block + 1 != me)
            def _():
                remote(
                    lent.at[block], got_before.at[me], send_sems.at[1], recv_sems.at[1], owner
                ).start()

            is_start = block == 0
            other = (jnp.where(is_start, before, tile), jnp.where(is_start, parts - 1, block - 1))

            @pl.when(block - 1 == me)
            def _():
                got_after[me] = lent[block]

            @pl.when(block - 1 != me)
            def _():
                remote(
                    lent.at[block], got_after.at[me], send_sems.at[2], recv_sems.at[2], other
                ).start()

        return 0

    lax.fori_loop(0, pairs, sums, 0)

    loads[5].wait()
    groups = cells_ref.shape[1] // LANES
    corner = jnp.concatenate(
        [
            cells_ref[k : k + 1, g * LANES : (g + 1) * LANES]
            for k in range(4)
            for g in range(groups)
        ],
        axis=0,
    )
    is_own = (corner >= width) & (corner < width + LANES)
    own_at = jnp.where(is_own, corner - width, 0)
    lent_at = jnp.where(is_own, 0, jnp.where(corner < width, corner, corner - LANES))

    def corners(own_row, lent_row):
        found = []
        for r in range(0, 4 * groups, ROWS):
            cut = slice(r, r + ROWS)
            found.append(
                jnp.where(
                    is_own[cut],
                    pick(jnp.broadcast_to(own_row, (ROWS, LANES)), own_at[cut]),
                    pick(jnp.broadcast_to(lent_row, (ROWS, LANES)), lent_at[cut]),
                )
            )
        whole = jnp.concatenate(found, axis=0)
        return [whole[k * groups : (k + 1) * groups] for k in range(4)]

    lane = lax.broadcasted_iota(jnp.int32, (ROWS, LANES), 1)
    is_before = lane < width

    @pl.when(is_first)
    def _():
        pltpu.make_async_copy(nodes.at[parts], nodes.at[parts], node_recv_sems.at[parts]).wait()

    @pl.when(is_last)
    def _():
        pltpu.make_async_copy(
            nodes.at[parts + 1], nodes.at[parts + 1], node_recv_sems.at[parts + 1]
        ).wait()

    slot_before = jnp.where(is_first, parts, me - 1)
    slot_after = jnp.where(is_last, parts + 1, me + 1)
    lent_nodes = jnp.where(
        is_before,
        lent_of(nodes[slot_before], slot_before),
        lent_of(nodes[slot_after], slot_after),
    )
    place = [corners(mine[k : k + 1], lent_nodes[k : k + 1]) for k in range(3)]

    bulk(got_own, parts - 1, recv_sems.at[0]).wait()
    own_totals = jnp.sum(got_own[...], axis=0)
    own_motion = node_shift(own_totals, mine)

    def wait_side(ref, is_edge, sem):
        @pl.when(is_edge)
        def _():
            bulk(ref, parts, sem).wait()

        @pl.when(jnp.logical_not(is_edge))
        def _():
            bulk(ref, parts - 1, sem).wait()

    wait_side(got_before, is_first, recv_sems.at[1])
    wait_side(got_after, is_last, recv_sems.at[2])
    lent_totals = jnp.where(
        is_before, jnp.sum(got_before[...], axis=0), jnp.sum(got_after[...], axis=0)
    )
    lent_motion = node_shift(lent_totals, lent_nodes)
    shift = [corners(own_motion[k], lent_motion[k]) for k in range(3)]

    half = [[place[k][c] + 0.5 * shift[k][c] for c in range(4)] for k in range(3)]
    swept = jnp.zeros((groups, LANES), jnp.float32)
    for first, second, third in FACES:
        normal = cross(
            [half[k][second] - half[k][first] for k in range(3)],
            [half[k][third] - half[k][first] for k in range(3)],
        )
        for k in range(3):
            swept = swept + (shift[k][first] + shift[k][second] + shift[k][third]) * normal[k]
    result_ref[0:3] = jnp.concatenate(own_motion, axis=0)
    result_ref[3 : 3 + groups] = swept * (1.0 / 6.0)

    bulk(nodes, parts - 1, node_send_sems.at[0]).wait()

    @pl.when(is_first)
    def _():
        bulk(nodes, 1, node_send_sems.at[1]).wait()

    @pl.when(is_last)
    def _():
        bulk(nodes, 1, node_send_sems.at[1]).wait()

    bulk(partial, parts - 1, send_sems.at[0]).wait()
    wait_side(lent, is_first, send_sems.at[1])
    wait_side(lent, is_last, send_sems.at[2])


def part_kernel(groups, result_ref, motion_ref, swept_ref):
    motion_ref[...] = result_ref[0:3]
    swept_ref[...] = result_ref[3 : 3 + groups]


def shards(tiles, parts, points, surface_points, displacement, rotation, halo_index, connectivity):
    width = halo_index.shape[0]
    depth = surface_points.shape[1]
    cells = connectivity.shape[1]
    groups = cells // LANES
    pair = 2 if parts % 2 == 0 else 1
    block = (ROWS, LANES)
    dma = pltpu.SemaphoreType.DMA
    result = pl.pallas_call(
        functools.partial(kernel, tiles, parts, width),
        out_shape=jax.ShapeDtypeStruct((-(-(3 + groups) // ROWS) * ROWS, LANES), jnp.float32),
        in_specs=[pl.BlockSpec(memory_space=pltpu.HBM)] * 6,
        out_specs=pl.BlockSpec(memory_space=pltpu.VMEM),
        scratch_shapes=[
            pltpu.VMEM((3, LANES), jnp.float32),
            pltpu.VMEM((3, depth), jnp.float32),
            pltpu.VMEM((3, depth), jnp.float32),
            pltpu.VMEM((3, depth), jnp.float32),
            pltpu.VMEM((1, width), jnp.int32),
            pltpu.VMEM((4, cells), jnp.int32),
            pltpu.VMEM((parts + 2, *block), jnp.float32),
            pltpu.VMEM((3, depth, LANES), jnp.float32),
            pltpu.VMEM((4 * ROWS, depth), jnp.bfloat16),
            pltpu.VMEM((depth, pair * LANES), jnp.bfloat16),
            pltpu.VMEM((depth, pair * LANES), jnp.bfloat16),
            pltpu.VMEM((parts, *block), jnp.float32),
            pltpu.VMEM((parts, *block), jnp.float32),
            pltpu.VMEM((parts, *block), jnp.float32),
            pltpu.VMEM((parts, *block), jnp.float32),
            pltpu.VMEM((parts, *block), jnp.float32),
            dma((6,)),
            dma((2,)),
            dma((parts + 2,)),
            dma((3,)),
            dma((3,)),
        ],
        compiler_params=pltpu.CompilerParams(
            collective_id=0, has_side_effects=True, vmem_limit_bytes=60 * 1024 * 1024
        ),
        cost_estimate=pl.CostEstimate(
            flops=2 * 7 * parts * LANES * depth,
            bytes_accessed=4 * (9 * depth + 4 * cells),
            transcendentals=parts * LANES * depth,
        ),
    )(points, surface_points, displacement, rotation, halo_index.reshape(1, width), connectivity)
    motion, swept = pl.pallas_call(
        functools.partial(part_kernel, groups),
        out_shape=(
            jax.ShapeDtypeStruct((3, LANES), jnp.float32),
            jax.ShapeDtypeStruct((groups, LANES), jnp.float32),
        ),
        in_specs=[pl.BlockSpec(memory_space=pltpu.VMEM)],
    )(result)
    return motion, swept.reshape(cells)


def solution(mesh):
    in_specs = (
        P(None, ("vol", "surf")),
        P(None, "surf"),
        P(None, "surf"),
        P(None, "surf"),
        P(("vol", "surf")),
        P(None, ("vol", "surf")),
    )
    out_specs = (P(None, ("vol", "surf")), P(("vol", "surf")))
    body = functools.partial(shards, mesh.shape["vol"], mesh.shape["surf"])
    return jax.shard_map(body, mesh=mesh, in_specs=in_specs, out_specs=out_specs, check_vma=False)
```

profile of v0, /device:TPU:0, one launch (start us, length us, event | category | flops | bytes accessed | tf_op | source)
XLA Modules:
  0.0 18.7 jit_solution(16433644853592688343)
XLA Ops:
  0.6 16.8 %shard_map.77.result_ref = f32[8,128]{1,0:T(8,128)} custom-call(f32[3,128]{1,0:T(4,128)} %points_in.1, f32[3,1024]{1,0:T(4,128)} %surface_in.1, f32[3,1024]{1,0:T(4,128)} %displacement_in.1, f32[3,1024]{1,0:T(4,128)} %rotation_in.1, s32[1,32]{1,0:T(1,128)} %bitcast.3, s32[4,512]{1,0:T(4,128)} %cells_in.1), custom_call_target="tpu_custom_call" | custom-call | flops 14680064 | bytes 45056 | tf_op jit(solution)/shard_map/pallas_call | solution.py:390
  17.5 1.3 %shard_map.78 = (f32[3,128]{1,0:T(4,128)}, f32[4,128]{1,0:T(4,128)}) custom-call(f32[8,128]{1,0:T(8,128)} %shard_map.77.result_ref), custom_call_target="tpu_custom_call" | custom-call | tf_op jit(solution)/shard_map/pallas_call | solution.py:427
where the time goes:
time: 18.9 us; the launch traced here: 18.7 us
  Pallas kernels  18.1 us (96%)
  between operations  0.64 us (3%)
    pallas_call x1, Pallas kernels, shards(): pl.pallas_call(functools.partial(kernel, tiles, parts, width), out_shape=...  16.8 us
    pallas_call x1, Pallas kernels, shards(): pl.pallas_call(functools.partial(part_kernel, groups), out_shape=(jax.Sha...  1.26 us

commit v1 on v0

--- a/solution.py
+++ b/solution.py
@@ -11,7 +11,7 @@
 LANES = 128
 ROWS = 8
 CHUNK = 256
-STEP = 32
+STEP = 64
 FACES = ((1, 2, 3), (0, 3, 2), (0, 1, 3), (0, 2, 1))
 MESH = pl.DeviceIdType.MESH
 
@@ -24,14 +24,33 @@
     )
 
 
-def split_rows(rows):
-    first = rows.astype(jnp.bfloat16)
-    rest = rows - first.astype(jnp.float32)
-    second = rest.astype(jnp.bfloat16)
-    third = rest - second.astype(jnp.float32)
-    return jnp.concatenate(
-        [first.astype(jnp.float32), second.astype(jnp.float32), third, jnp.zeros_like(rows)], axis=0
-    ).astype(jnp.bfloat16)
+def three_terms(rows):
+    first = rows.astype(jnp.bfloat16).astype(jnp.float32)
+    rest = rows - first
+    second = rest.astype(jnp.bfloat16).astype(jnp.float32)
+    return first, second, (rest - second).astype(jnp.bfloat16).astype(jnp.float32)
+
+
+def stack(*blocks):
+    return jnp.concatenate(blocks, axis=0)
+
+
+def node_factors(rows):
+    x, y, z = rows[0:1], rows[1:2], rows[2:3]
+    ones = jnp.ones_like(x)
+    first, second, third = three_terms(
+        stack(-2.0 * x, -2.0 * y, -2.0 * z, x * x + y * y + z * z, ones, 0.0 * ones, 0.0 * ones, 0.0 * ones)
+    )
+    return stack(first, first, second, second, first, third)
+
+
+def surface_factors(rows):
+    x, y, z = rows[0:1], rows[1:2], rows[2:3]
+    ones = jnp.ones_like(x)
+    first, second, third = three_terms(
+        stack(x, y, z, ones, x * x + y * y + (z * z + SOFTENING), 0.0 * ones, 0.0 * ones, 0.0 * ones)
+    )
+    return stack(first, second, first, second, third, first)
 
 
 def pick(rows, index):
@@ -54,7 +73,8 @@
     rotation_in,
     halo_in,
     cells_in,
-    result_ref,
+    motion_out,
+    swept_out,
     points_ref,
     surface_ref,
     displacement_ref,
@@ -71,6 +91,8 @@
     got_own,
     got_before,
     got_after,
+    motion_ref,
+    swept_ref,
     load_sems,
     node_send_sems,
     node_recv_sems,
@@ -179,14 +201,11 @@
         ],
         axis=0,
     )
-    terms[...] = split_rows(rows)
-    padded = jnp.concatenate([surface, jnp.zeros((ROWS - 3, depth), jnp.float32)], axis=0)
+    terms[...] = stack(*three_terms(rows), jnp.zeros_like(rows)).astype(jnp.bfloat16)
+    factors = surface_factors(surface)
     for start in range(0, depth, LANES):
-        upright = padded[:, start : start + LANES].T
-        for k in range(3):
-            anchors[k, start : start + LANES] = jnp.broadcast_to(
-                upright[:, k : k + 1], (LANES, LANES)
-            )
+        cut = slice(start, start + LANES)
+        anchors[cut] = factors[:, cut].T.astype(jnp.bfloat16)
 
     def lent_of(values, slot):
         index = jnp.broadcast_to(nodes[slot][3:4], (ROWS, LANES)).astype(jnp.int32)
@@ -206,22 +225,19 @@
                     nodes.at[base + k], nodes.at[base + k], node_recv_sems.at[base + k]
                 ).wait()
 
-        places = [nodes[base + k] for k in range(pair)]
+        places = jnp.concatenate(
+            [node_factors(nodes[base + k]) for k in range(pair)], axis=1
+        ).astype(jnp.bfloat16)
         total = jnp.zeros((4 * ROWS, pair * LANES), jnp.float32)
         for start in range(0, depth, CHUNK):
             for row in range(start, start + CHUNK, STEP):
                 cut = slice(row, row + STEP)
-                sx, sy, sz = anchors[0, cut], anchors[1, cut], anchors[2, cut]
-                for k in range(pair):
-                    gx = sx - places[k][0:1]
-                    gy = sy - places[k][1:2]
-                    gz = sz - places[k][2:3]
-                    root = lax.rsqrt(gx * gx + gy * gy + (gz * gz + SOFTENING))
-                    weight = root * root * root
-                    top = weight.astype(jnp.bfloat16)
-                    side = slice(k * LANES, (k + 1) * LANES)
-                    high[cut, side] = top
-                    low[cut, side] = (weight - top.astype(jnp.float32)).astype(jnp.bfloat16)
+                spread = jnp.dot(anchors[cut], places, preferred_element_type=jnp.float32)
+                root = lax.rsqrt(spread)
+                weight = root * root * root
+                top = weight.astype(jnp.bfloat16)
+                high[cut] = top
+                low[cut] = (weight - top.astype(jnp.float32)).astype(jnp.bfloat16)
             cut = slice(start, start + CHUNK)
             left = terms[:, cut]
             total = total + jnp.dot(left, high[cut], preferred_element_type=jnp.float32)
@@ -329,6 +345,9 @@
     bulk(got_own, parts - 1, recv_sems.at[0]).wait()
     own_totals = jnp.sum(got_own[...], axis=0)
     own_motion = node_shift(own_totals, mine)
+    motion_ref[...] = jnp.concatenate(own_motion, axis=0)
+    save_motion = pltpu.make_async_copy(motion_ref, motion_out, load_sems.at[6])
+    save_motion.start()
 
     def wait_side(ref, is_edge, sem):
         @pl.when(is_edge)
@@ -356,8 +375,9 @@
         )
         for k in range(3):
             swept = swept + (shift[k][first] + shift[k][second] + shift[k][third]) * normal[k]
-    result_ref[0:3] = jnp.concatenate(own_motion, axis=0)
-    result_ref[3 : 3 + groups] = swept * (1.0 / 6.0)
+    swept_ref[...] = swept * (1.0 / 6.0)
+    save_swept = pltpu.make_async_copy(swept_ref, swept_out, load_sems.at[7])
+    save_swept.start()
 
     bulk(nodes, parts - 1, node_send_sems.at[0]).wait()
 
@@ -372,11 +392,19 @@
     bulk(partial, parts - 1, send_sems.at[0]).wait()
     wait_side(lent, is_first, send_sems.at[1])
     wait_side(lent, is_last, send_sems.at[2])
-
-
-def part_kernel(groups, result_ref, motion_ref, swept_ref):
-    motion_ref[...] = result_ref[0:3]
-    swept_ref[...] = result_ref[3 : 3 + groups]
+    save_motion.wait()
+    save_swept.wait()
+
+
+def hand_on(motion_in, swept_in, motion_out, swept_out, sems):
+    copies = [
+        pltpu.make_async_copy(motion_in, motion_out, sems.at[0]),
+        pltpu.make_async_copy(swept_in, swept_out, sems.at[1]),
+    ]
+    for copy in copies:
+        copy.start()
+    for copy in copies:
+        copy.wait()
 
 
 def shards(tiles, parts, points, surface_points, displacement, rotation, halo_index, connectivity):
@@ -387,11 +415,15 @@
     pair = 2 if parts % 2 == 0 else 1
     block = (ROWS, LANES)
     dma = pltpu.SemaphoreType.DMA
-    result = pl.pallas_call(
+    outputs = (
+        jax.ShapeDtypeStruct((3, LANES), jnp.float32),
+        jax.ShapeDtypeStruct((groups, LANES), jnp.float32),
+    )
+    motion, swept = pl.pallas_call(
         functools.partial(kernel, tiles, parts, width),
-        out_shape=jax.ShapeDtypeStruct((-(-(3 + groups) // ROWS) * ROWS, LANES), jnp.float32),
+        out_shape=outputs,
         in_specs=[pl.BlockSpec(memory_space=pltpu.HBM)] * 6,
-        out_specs=pl.BlockSpec(memory_space=pltpu.VMEM),
+        out_specs=(pl.BlockSpec(memory_space=pl.ANY),) * 2,
         scratch_shapes=[
             pltpu.VMEM((3, LANES), jnp.float32),
             pltpu.VMEM((3, depth), jnp.float32),
@@ -400,7 +432,7 @@
             pltpu.VMEM((1, width), jnp.int32),
             pltpu.VMEM((4, cells), jnp.int32),
             pltpu.VMEM((parts + 2, *block), jnp.float32),
-            pltpu.VMEM((3, depth, LANES), jnp.float32),
+            pltpu.VMEM((depth, 6 * ROWS), jnp.bfloat16),
             pltpu.VMEM((4 * ROWS, depth), jnp.bfloat16),
             pltpu.VMEM((depth, pair * LANES), jnp.bfloat16),
             pltpu.VMEM((depth, pair * LANES), jnp.bfloat16),
@@ -409,7 +441,9 @@
             pltpu.VMEM((parts, *block), jnp.float32),
             pltpu.VMEM((parts, *block), jnp.float32),
             pltpu.VMEM((parts, *block), jnp.float32),
-            dma((6,)),
+            pltpu.VMEM((3, LANES), jnp.float32),
+            pltpu.VMEM((groups, LANES), jnp.float32),
+            dma((8,)),
             dma((2,)),
             dma((parts + 2,)),
             dma((3,)),
@@ -425,13 +459,13 @@
         ),
     )(points, surface_points, displacement, rotation, halo_index.reshape(1, width), connectivity)
     motion, swept = pl.pallas_call(
-        functools.partial(part_kernel, groups),
-        out_shape=(
-            jax.ShapeDtypeStruct((3, LANES), jnp.float32),
-            jax.ShapeDtypeStruct((groups, LANES), jnp.float32),
-        ),
-        in_specs=[pl.BlockSpec(memory_space=pltpu.VMEM)],
-    )(result)
+        hand_on,
+        out_shape=outputs,
+        in_specs=[pl.BlockSpec(memory_space=pl.ANY)] * 2,
+        out_specs=(pl.BlockSpec(memory_space=pl.ANY),) * 2,
+        scratch_shapes=[dma((2,))],
+        compiler_params=pltpu.CompilerParams(vmem_limit_bytes=60 * 1024 * 1024),
+    )(motion, swept)
     return motion, swept.reshape(cells)
 
 

time: 18.9 us -> 18.6 us (0.984)
  Pallas kernels: 18.1 us -> 17.8 us
    pallas_call x1, Pallas kernels: 16.8 us -> 16.5 us  [shards(): pl.pallas_call(functools.partial(kernel, tiles, parts, width), out_shape=...]
where the time goes in v1:
time: 18.6 us; the launch traced here: 18.4 us
  Pallas kernels  17.8 us (96%)
  between operations  0.64 us (3%)
    pallas_call x1, Pallas kernels, shards(): pl.pallas_call(functools.partial(kernel, tiles, parts, width), out_shape=...  16.5 us
    pallas_call x1, Pallas kernels, shards(): pl.pallas_call(hand_on, out_shape=outputs, in_specs=[pl.BlockSpec(memory_...  1.23 us

profile of v1, /device:TPU:0, one launch (start us, length us, event | category | flops | bytes accessed | tf_op | source)
XLA Modules:
  0.0 18.4 jit_solution(16503704185451650245)
XLA Ops:
  0.6 16.5 %shard_map.77 = (f32[3,128]{1,0:T(4,128)}, f32[4,128]{1,0:T(4,128)}) custom-call(f32[3,128]{1,0:T(4,128)} %points_in.1, f32[3,1024]{1,0:T(4,128)} %surface_in.1, f32[3,1024]{1,0:T(4,128)} %displacement_in.1, f32[3,1024]{1,0:T(4,128)} %rotation_in.1, s32[1,32]{1,0:T(1,128)} %bitcast.3, s32[4,512]{1,0:T(4,128)} %cells_in.1), custom_call_target="tpu_custom_call" | custom-call | flops 14680064 | bytes 45056 | tf_op jit(solution)/shard_map/pallas_call | solution.py:422
  17.2 1.2 %shard_map.78 = (f32[3,128]{1,0:T(4,128)}, f32[4,128]{1,0:T(4,128)}) custom-call(f32[3,128]{1,0:T(4,128)} %get-tuple-element.6.motion_in, f32[4,128]{1,0:T(4,128)} %get-tuple-element.7.swept_in), custom_call_target="tpu_custom_call" | custom-call | tf_op jit(solution)/shard_map/pallas_call | solution.py:461

commit v2 on v1

--- a/solution.py
+++ b/solution.py
@@ -73,8 +73,8 @@
     rotation_in,
     halo_in,
     cells_in,
-    motion_out,
-    swept_out,
+    motion_ref,
+    swept_ref,
     points_ref,
     surface_ref,
     displacement_ref,
@@ -86,13 +86,9 @@
     terms,
     high,
     low,
-    partial,
-    lent,
-    got_own,
-    got_before,
-    got_after,
-    motion_ref,
-    swept_ref,
+    staged,
+    got_pair,
+    got_side,
     load_sems,
     node_send_sems,
     node_recv_sems,
@@ -160,30 +156,6 @@
         [points_ref[...], halo_row, jnp.zeros((ROWS - 4, LANES), jnp.float32)], axis=0
     )
     nodes[me] = mine
-    pl.semaphore_wait(barrier, parts + 1)
-
-    def share(step, _):
-        other = lax.rem(me + step, parts)
-        remote(
-            nodes.at[me], nodes.at[me], node_send_sems.at[0], node_recv_sems.at[me], (tile, other)
-        ).start()
-        return 0
-
-    lax.fori_loop(1, parts, share, 0)
-
-    def share_far(slot, device):
-        remote(
-            nodes.at[me], nodes.at[slot], node_send_sems.at[1], node_recv_sems.at[slot], device
-        ).start()
-
-    @pl.when(is_last)
-    def _():
-        share_far(parts, (after, 0))
-
-    @pl.when(is_first)
-    def _():
-        share_far(parts + 1, (before, parts - 1))
-
     for load in loads[2:5]:
         load.wait()
     depth = surface_ref.shape[1]
@@ -207,11 +179,35 @@
         cut = slice(start, start + LANES)
         anchors[cut] = factors[:, cut].T.astype(jnp.bfloat16)
 
+    pl.semaphore_wait(barrier, parts + 1)
+
+    def share(step, _):
+        other = lax.rem(me + step, parts)
+        remote(
+            nodes.at[me], nodes.at[me], node_send_sems.at[0], node_recv_sems.at[me], (tile, other)
+        ).start()
+        return 0
+
+    lax.fori_loop(1, parts, share, 0)
+
+    def share_far(slot, device):
+        remote(
+            nodes.at[me], nodes.at[slot], node_send_sems.at[1], node_recv_sems.at[slot], device
+        ).start()
+
+    @pl.when(is_last)
+    def _():
+        share_far(parts, (after, 0))
+
+    @pl.when(is_first)
+    def _():
+        share_far(parts + 1, (before, parts - 1))
+
     def lent_of(values, slot):
         index = jnp.broadcast_to(nodes[slot][3:4], (ROWS, LANES)).astype(jnp.int32)
         return pick(values, index)
 
-    pair = 2 if parts % 2 == 0 else 1
+    pair = 2
     pairs = parts // pair
     turn = 1 - 2 * jnp.minimum((me // pair) // max(pairs // 2, 1), 1)
 
@@ -243,54 +239,47 @@
             total = total + jnp.dot(left, high[cut], preferred_element_type=jnp.float32)
             total = total + jnp.dot(left, low[cut], preferred_element_type=jnp.float32)
         added = total[0:ROWS] + total[ROWS : 2 * ROWS] + total[2 * ROWS : 3 * ROWS]
-        halves = [added[:, k * LANES : (k + 1) * LANES] for k in range(pair)]
-        for k in range(pair):
-            partial[base + k] = halves[k]
-        for k in range(pair):
-            lent[base + k] = lent_of(halves[k], base + k)
-        for k in range(pair):
+        halves = [added[:, 0:LANES], added[:, LANES:]]
+        for k in range(2):
+            staged[base + k, 0] = halves[k]
+            staged[base + 1 - k, 1] = lent_of(halves[k], base + k)
+        for k in range(2):
             block = base + k
-            is_mine = block == me
-
-            @pl.when(is_mine)
-            def _():
-                got_own[me] = halves[k]
-
-            @pl.when(jnp.logical_not(is_mine))
+
+            @pl.when(block != me)
             def _():
                 remote(
-                    partial.at[block], got_own.at[me], send_sems.at[0], recv_sems.at[0], (tile, block)
+                    staged.at[block], got_pair.at[me], send_sems.at[0], recv_sems.at[0], (tile, block)
                 ).start()
 
-            is_end = block == parts - 1
-            owner = (jnp.where(is_end, after, tile), jnp.where(is_end, 0, block + 1))
-
-            @pl.when(block + 1 == me)
-            def _():
-                got_before[me] = lent[block]
-
-            @pl.when(block + 1 != me)
+        is_start = base == 0
+        is_end = base == parts - 2
+        sides = (
+            (1, base - 1, jnp.where(is_start, before, tile), jnp.where(is_start, parts - 1, base - 1)),
+            (0, base + 2, jnp.where(is_end, after, tile), jnp.where(is_end, 0, base + 2)),
+        )
+        for k, block, owner_tile, owner in sides:
+
+            @pl.when(block != me)
             def _():
                 remote(
-                    lent.at[block], got_before.at[me], send_sems.at[1], recv_sems.at[1], owner
+                    staged.at[base + k, 1],
+                    got_side.at[me],
+                    send_sems.at[1],
+                    recv_sems.at[1],
+                    (owner_tile, owner),
                 ).start()
 
-            is_start = block == 0
-            other = (jnp.where(is_start, before, tile), jnp.where(is_start, parts - 1, block - 1))
-
-            @pl.when(block - 1 == me)
-            def _():
-                got_after[me] = lent[block]
-
-            @pl.when(block - 1 != me)
-            def _():
-                remote(
-                    lent.at[block], got_after.at[me], send_sems.at[2], recv_sems.at[2], other
-                ).start()
-
         return 0
 
     lax.fori_loop(0, pairs, sums, 0)
+    got_pair[me] = staged[me]
+    is_odd = lax.rem(me, 2)
+    is_edge = is_first | is_last
+
+    @pl.when(jnp.logical_not(is_edge))
+    def _():
+        got_side[me] = staged[me - 2 + 4 * is_odd, 1]
 
     loads[5].wait()
     groups = cells_ref.shape[1] // LANES
@@ -342,14 +331,13 @@
     )
     place = [corners(mine[k : k + 1], lent_nodes[k : k + 1]) for k in range(3)]
 
-    bulk(got_own, parts - 1, recv_sems.at[0]).wait()
-    own_totals = jnp.sum(got_own[...], axis=0)
+    bulk(got_pair, parts - 1, recv_sems.at[0]).wait()
+    own_totals = jnp.sum(got_pair[:, 0], axis=0)
+    near_totals = jnp.sum(got_pair[:, 1], axis=0)
     own_motion = node_shift(own_totals, mine)
     motion_ref[...] = jnp.concatenate(own_motion, axis=0)
-    save_motion = pltpu.make_async_copy(motion_ref, motion_out, load_sems.at[6])
-    save_motion.start()
-
-    def wait_side(ref, is_edge, sem):
+
+    def wait_side(ref, sem):
         @pl.when(is_edge)
         def _():
             bulk(ref, parts, sem).wait()
@@ -358,11 +346,10 @@
         def _():
             bulk(ref, parts - 1, sem).wait()
 
-    wait_side(got_before, is_first, recv_sems.at[1])
-    wait_side(got_after, is_last, recv_sems.at[2])
-    lent_totals = jnp.where(
-        is_before, jnp.sum(got_before[...], axis=0), jnp.sum(got_after[...], axis=0)
-    )
+    wait_side(got_side, recv_sems.at[1])
+    side_totals = jnp.sum(got_side[...], axis=0)
+    from_near = (lane >= width) == (jnp.broadcast_to(is_odd, (ROWS, LANES)) == 0)
+    lent_totals = jnp.where(from_near, near_totals, side_totals)
     lent_motion = node_shift(lent_totals, lent_nodes)
     shift = [corners(own_motion[k], lent_motion[k]) for k in range(3)]
 
@@ -376,8 +363,6 @@
         for k in range(3):
             swept = swept + (shift[k][first] + shift[k][second] + shift[k][third]) * normal[k]
     swept_ref[...] = swept * (1.0 / 6.0)
-    save_swept = pltpu.make_async_copy(swept_ref, swept_out, load_sems.at[7])
-    save_swept.start()
 
     bulk(nodes, parts - 1, node_send_sems.at[0]).wait()
 
@@ -389,11 +374,8 @@
     def _():
         bulk(nodes, 1, node_send_sems.at[1]).wait()
 
-    bulk(partial, parts - 1, send_sems.at[0]).wait()
-    wait_side(lent, is_first, send_sems.at[1])
-    wait_side(lent, is_last, send_sems.at[2])
-    save_motion.wait()
-    save_swept.wait()
+    bulk(staged, parts - 1, send_sems.at[0]).wait()
+    wait_side(got_side, send_sems.at[1])
 
 
 def hand_on(motion_in, swept_in, motion_out, swept_out, sems):
@@ -412,9 +394,17 @@
     depth = surface_points.shape[1]
     cells = connectivity.shape[1]
     groups = cells // LANES
-    pair = 2 if parts % 2 == 0 else 1
+    pair = 2
     block = (ROWS, LANES)
     dma = pltpu.SemaphoreType.DMA
+    inputs = (
+        points,
+        surface_points,
+        displacement,
+        rotation,
+        halo_index.reshape(1, width),
+        connectivity,
+    )
     outputs = (
         jax.ShapeDtypeStruct((3, LANES), jnp.float32),
         jax.ShapeDtypeStruct((groups, LANES), jnp.float32),
@@ -423,7 +413,7 @@
         functools.partial(kernel, tiles, parts, width),
         out_shape=outputs,
         in_specs=[pl.BlockSpec(memory_space=pltpu.HBM)] * 6,
-        out_specs=(pl.BlockSpec(memory_space=pl.ANY),) * 2,
+        out_specs=(pl.BlockSpec(memory_space=pltpu.VMEM),) * 2,
         scratch_shapes=[
             pltpu.VMEM((3, LANES), jnp.float32),
             pltpu.VMEM((3, depth), jnp.float32),
@@ -436,35 +426,30 @@
             pltpu.VMEM((4 * ROWS, depth), jnp.bfloat16),
             pltpu.VMEM((depth, pair * LANES), jnp.bfloat16),
             pltpu.VMEM((depth, pair * LANES), jnp.bfloat16),
+            pltpu.VMEM((parts, 2, *block), jnp.float32),
+            pltpu.VMEM((parts, 2, *block), jnp.float32),
             pltpu.VMEM((parts, *block), jnp.float32),
-            pltpu.VMEM((parts, *block), jnp.float32),
-            pltpu.VMEM((parts, *block), jnp.float32),
-            pltpu.VMEM((parts, *block), jnp.float32),
-            pltpu.VMEM((parts, *block), jnp.float32),
-            pltpu.VMEM((3, LANES), jnp.float32),
-            pltpu.VMEM((groups, LANES), jnp.float32),
-            dma((8,)),
+            dma((6,)),
             dma((2,)),
             dma((parts + 2,)),
-            dma((3,)),
-            dma((3,)),
+            dma((2,)),
+            dma((2,)),
         ],
         compiler_params=pltpu.CompilerParams(
-            collective_id=0, has_side_effects=True, vmem_limit_bytes=60 * 1024 * 1024
+            collective_id=0, has_side_effects=True, vmem_limit_bytes=16 * 1024 * 1024
         ),
         cost_estimate=pl.CostEstimate(
             flops=2 * 7 * parts * LANES * depth,
             bytes_accessed=4 * (9 * depth + 4 * cells),
             transcendentals=parts * LANES * depth,
         ),
-    )(points, surface_points, displacement, rotation, halo_index.reshape(1, width), connectivity)
+    )(*(pltpu.with_memory_space_constraint(array, pltpu.HBM) for array in inputs))
     motion, swept = pl.pallas_call(
         hand_on,
         out_shape=outputs,
-        in_specs=[pl.BlockSpec(memory_space=pl.ANY)] * 2,
+        in_specs=[pl.BlockSpec(memory_space=pltpu.VMEM)] * 2,
         out_specs=(pl.BlockSpec(memory_space=pl.ANY),) * 2,
         scratch_shapes=[dma((2,))],
-        compiler_params=pltpu.CompilerParams(vmem_limit_bytes=60 * 1024 * 1024),
     )(motion, swept)
     return motion, swept.reshape(cells)
 

time: 18.6 us -> 19.1 us (1.027)
  local copies, waits for them, and re-layouts: 0 us -> 1.13 us
  Pallas kernels: 17.8 us -> 17.1 us
    unnamed x0 -> x4, local copies, waits for them, and re-layouts: none -> 1.13 us
    pallas_call x1, Pallas kernels: 16.5 us -> 15.8 us  [shards(): pl.pallas_call(functools.partial(kernel, tiles, parts, width), out_shape=...]
where the time goes in v2:
time: 19.1 us; the launch traced here: 18.9 us
  Pallas kernels  17.1 us (90%)
  local copies, waits for them, and re-layouts  1.13 us (6%)
  between operations  0.65 us (3%)
    pallas_call x1, Pallas kernels, shards(): pl.pallas_call(functools.partial(kernel, tiles, parts, width), out_shape=...  15.8 us
    pallas_call x1, Pallas kernels, shards(): pl.pallas_call(hand_on, out_shape=outputs, in_specs=[pl.BlockSpec(memory_...  1.27 us
    unnamed x4, local copies, waits for them, and re-layouts  1.13 us

profile of v2, /device:TPU:0, one launch (start us, length us, event | category | flops | bytes accessed | tf_op | source)
XLA Modules:
  0.0 18.9 jit_solution(16902686355232977033)
XLA Ops:
  0.6 15.8 %shard_map.77 = (f32[3,128]{1,0:T(4,128)S(1)}, f32[4,128]{1,0:T(4,128)S(1)}) custom-call(f32[3,128]{1,0:T(4,128)} %points_in.1, f32[3,1024]{1,0:T(4,128)} %surface_in.1, f32[3,1024]{1,0:T(4,128)} %displacement_in.1, f32[3,1024]{1,0:T(4,128)} %rotation_in.1, s32[1,32]{1,0:T(1,128)} %bitcast.3, s32[4,512]{1,0:T(4,128)} %cells_in.1), custom_call_target="tpu_custom_call" | custom-call | flops 14680064 | bytes 45056 | tf_op jit(solution)/shard_map/pallas_call | solution.py:412
  16.5 0.0 copy-start
  16.5 0.6 %copy-done = f32[3,128]{1,0:T(4,128)} copy-done((f32[3,128]{1,0:T(4,128)}, f32[3,128]{1,0:T(4,128)S(1)}, u32[]{:S(2)}) %copy-start) | copy-done | bytes 1560
  17.0 0.0 copy-start.1
  17.0 0.6 %copy-done.1 = f32[4,128]{1,0:T(4,128)} copy-done((f32[4,128]{1,0:T(4,128)}, f32[4,128]{1,0:T(4,128)S(1)}, u32[]{:S(2)}) %copy-start.1) | copy-done | bytes 2072
  17.6 1.3 %shard_map.78 = (f32[3,128]{1,0:T(4,128)}, f32[4,128]{1,0:T(4,128)}) custom-call(f32[3,128]{1,0:T(4,128)} %copy-done, f32[4,128]{1,0:T(4,128)} %copy-done.1), custom_call_target="tpu_custom_call" | custom-call | tf_op jit(solution)/shard_map/pallas_call | solution.py:447
Async XLA Ops:
  16.5 0.6 %copy-start = (f32[3,128]{1,0:T(4,128)}, f32[3,128]{1,0:T(4,128)S(1)}, u32[]{:S(2)}) copy-start(f32[3,128]{1,0:T(4,128)S(1)} %get-tuple-element.6.motion_in) | copy-start | bytes 4612
  17.0 0.6 %copy-start.1 = (f32[4,128]{1,0:T(4,128)}, f32[4,128]{1,0:T(4,128)S(1)}, u32[]{:S(2)}) copy-start(f32[4,128]{1,0:T(4,128)S(1)} %get-tuple-element.7.swept_in) | copy-start | bytes 6148

commit v3 on v2

--- a/solution.py
+++ b/solution.py
@@ -11,7 +11,7 @@
 LANES = 128
 ROWS = 8
 CHUNK = 256
-STEP = 64
+STEP = 256
 FACES = ((1, 2, 3), (0, 3, 2), (0, 1, 3), (0, 2, 1))
 MESH = pl.DeviceIdType.MESH
 
@@ -450,6 +450,7 @@
         in_specs=[pl.BlockSpec(memory_space=pltpu.VMEM)] * 2,
         out_specs=(pl.BlockSpec(memory_space=pl.ANY),) * 2,
         scratch_shapes=[dma((2,))],
+        compiler_params=pltpu.CompilerParams(vmem_limit_bytes=1024 * 1024),
     )(motion, swept)
     return motion, swept.reshape(cells)
 

time: 19.1 us -> 17.1 us (0.90)
  local copies, waits for them, and re-layouts: 1.13 us -> 0 us
  Pallas kernels: 17.1 us -> 16.3 us
    unnamed x4 -> x0, local copies, waits for them, and re-layouts: 1.13 us -> none
    pallas_call x1, Pallas kernels: 1.27 us -> 0.6 us  [shards(): pl.pallas_call(hand_on, out_shape=outputs, in_specs=[pl.BlockSpec(memory_...]
where the time goes in v3:
time: 17.1 us; the launch traced here: 17 us
  Pallas kernels  16.3 us (95%)
  between operations  0.64 us (4%)
    pallas_call x1, Pallas kernels, shards(): pl.pallas_call(functools.partial(kernel, tiles, parts, width), out_shape=...  15.7 us
    pallas_call x1, Pallas kernels, shards(): pl.pallas_call(hand_on, out_shape=outputs, in_specs=[pl.BlockSpec(memory_...  0.6 us

profile of v3, /device:TPU:0, one launch (start us, length us, event | category | flops | bytes accessed | tf_op | source)
XLA Modules:
  0.0 17.0 jit_solution(1482868035060781444)
XLA Ops:
  0.6 15.7 %shard_map.77 = (f32[3,128]{1,0:T(4,128)S(1)}, f32[4,128]{1,0:T(4,128)S(1)}) custom-call(f32[3,128]{1,0:T(4,128)} %points_in.1, f32[3,1024]{1,0:T(4,128)} %surface_in.1, f32[3,1024]{1,0:T(4,128)} %displacement_in.1, f32[3,1024]{1,0:T(4,128)} %rotation_in.1, s32[1,32]{1,0:T(1,128)} %bitcast.3, s32[4,512]{1,0:T(4,128)} %cells_in.1), custom_call_target="tpu_custom_call" | custom-call | flops 14680064 | bytes 45056 | tf_op jit(solution)/shard_map/pallas_call | solution.py:412
  16.4 0.6 %shard_map.78 = (f32[3,128]{1,0:T(4,128)}, f32[4,128]{1,0:T(4,128)}) custom-call(f32[3,128]{1,0:T(4,128)S(1)} %get-tuple-element.6.motion_in, f32[4,128]{1,0:T(4,128)S(1)} %get-tuple-element.7.swept_in), custom_call_target="tpu_custom_call" | custom-call | tf_op jit(solution)/shard_map/pallas_call | solution.py:447
